TPU v7x, 256 devices: a whole 4x4x8 slice. The times are simulated.
256 devices in a mesh: section: 4 (over z_lo), expert: 16 (over x, y), dp: 4 (over z_hi, core).
Axes of the slice: x: 4, y: 4, z: 8 (z_hi: 2, z_lo: 4; z = z_hi * 4 + z_lo), core: 2. Of those that a mesh axis runs over, the one named last changes fastest.
Arguments:
- inputs: bfloat16 [4, 512, 2048], P(None, 'expert'), may hold values from -6 to 6
- norm_gain: bfloat16 [4, 2048], P('section'), may hold values from 0.099609375 to 1.8984375
- gate_weight: bfloat16 [4, 2048, 49152], P('section', None, ('expert', 'dp')), may hold values from -0.125 to 0.125
- up_weight: bfloat16 [4, 2048, 49152], P('section', None, ('expert', 'dp')), may hold values from -0.125 to 0.125
- down_weight: bfloat16 [4, 49152, 2048], P('section', ('expert', 'dp')), may hold values from -0.0546875 to 0.0546875
- expert_ids: int32 [4, 4, 512, 1], P('section', None, 'expert'), may hold values from 0 to 3; in each aligned block of 32 rows (0 to 31, 32 to 63, ..., all dimensions but the last counted through in order) at most 12 rows name the same one
Outputs:
- layer_outputs: bfloat16 [4, 4, 512, 2048], P('section', None, 'expert')
Inputs may be any that keep to these rules, and one draw needn't show every extreme that they name: `expert_ids`: among the 32 tokens of one device for one layer and block, no expert is named more than 12 times.
All inputs are finite; a program needn't handle non-finite values.
Results may differ from a plain program's by a relative error of at most 0.03.
Values may be sent and summed in bfloat16 or wider, within the bound.
A program may use at most 64 MiB of HBM per device.

v0:
```python
import jax
import jax.numpy as jnp
from jax import lax
from jax.sharding import PartitionSpec as P


def from_behind(value, axis, steps):
    count = lax.axis_size(axis)
    initial, last = (max(0, -steps), min(count, count - steps))
    return lax.ppermute(value, axis, [(source, source + steps) for source in range(initial, last)])


def shards(inputs, norm_gain, gate_weight, up_weight, down_weight, expert_ids):
    n_expert = lax.axis_size("expert")
    n_section = lax.axis_size("section")
    experts = min(n_expert, 4)
    split = n_expert // experts
    spans, tok, width = inputs.shape
    capacity = tok // experts * 3 // 2
    section = lax.axis_index("section")
    tri = (
        lax.broadcasted_iota(jnp.int32, (tok, tok), 0)
        > lax.broadcasted_iota(jnp.int32, (tok, tok), 1)
    ).astype(jnp.float32)
    gain = norm_gain[0].astype(jnp.float32)
    w_gate = gate_weight[0]
    w_up = up_weight[0]
    w_down = down_weight[0]
    saved = jnp.zeros((1, spans, tok, width), jnp.bfloat16)
    carried = jnp.zeros((tok, width), jnp.bfloat16)
    for step in range(spans + n_section - 1):
        if step > 0:
            carried = from_behind(carried, "section", 1)
        position = step - section
        index = jnp.clip(position, 0, spans - 1)
        fresh = inputs[min(step, spans - 1)]
        stream = jnp.where(section == 0, fresh, carried)
        ids_now = lax.dynamic_index_in_dim(expert_ids[0], index, 0, keepdims=False)[:, 0]
        hf = stream.astype(jnp.float32)
        scale = lax.rsqrt(jnp.mean(hf * hf, axis=-1, keepdims=True) + 1e-05)
        normed = (hf * scale * gain).astype(jnp.bfloat16)
        onehot = (ids_now[:, None] == lax.broadcasted_iota(jnp.int32, (tok, experts), 1)).astype(
            jnp.float32
        )
        earlier = jnp.dot(tri, onehot, precision=lax.Precision.HIGHEST)
        rank = jnp.sum(earlier * onehot, axis=1)
        slots = (
            rank[:, None] == lax.broadcasted_iota(jnp.int32, (tok, capacity), 1).astype(jnp.float32)
        ).astype(jnp.float32)
        place = jnp.einsum("te,tc->ect", onehot, slots).astype(jnp.bfloat16)
        place_all = jnp.repeat(place, split, axis=0)
        buffer = jnp.einsum(
            "ect,td->ecd", place, normed, preferred_element_type=jnp.float32
        ).astype(jnp.bfloat16)
        outgoing = jnp.repeat(buffer, split, axis=0)
        arrived = lax.all_to_all(outgoing, "expert", split_axis=0, concat_axis=0, tiled=True)
        rows = arrived.reshape(n_expert * capacity, width)
        gate = jnp.dot(rows, w_gate, preferred_element_type=jnp.float32)
        upper = jnp.dot(rows, w_up, preferred_element_type=jnp.float32)
        active = (jax.nn.silu(gate) * upper).astype(jnp.bfloat16)
        partial_value = jnp.dot(active, w_down, preferred_element_type=jnp.float32).reshape(
            n_expert, capacity, width
        )
        rounded = partial_value.astype(jnp.bfloat16)
        returned = lax.all_to_all(rounded, "expert", split_axis=0, concat_axis=0, tiled=True)
        local_sum = jnp.einsum(
            "jct,jcd->td", place_all, returned, preferred_element_type=jnp.float32
        )
        update = lax.psum(local_sum.astype(jnp.bfloat16), "dp").astype(jnp.float32)
        result = (hf + update).astype(jnp.bfloat16)
        valid = (position >= 0) & (position < spans)
        current = lax.dynamic_index_in_dim(saved[0], index, 0, keepdims=False)
        kept = jnp.where(valid, result, current)
        zero = jnp.zeros((), jnp.int32)
        saved = lax.dynamic_update_slice(saved, kept[None, None], (zero, index, zero, zero))
        carried = result
    return saved


def solution(mesh):
    placed = (
        P(None, "expert", None),
        P("section", None),
        P("section", None, ("expert", "dp")),
        P("section", None, ("expert", "dp")),
        P("section", ("expert", "dp"), None),
        P("section", None, "expert", None),
    )
    return jax.shard_map(
        shards,
        mesh=mesh,
        in_specs=placed,
        out_specs=P("section", None, "expert", None),
        check_vma=False,
    )
```

profile of v0, /device:TPU:97, one launch (start us, length us, event | category | flops | bytes accessed | tf_op | source)
XLA Modules:
  0.0 813.3 jit_solution(9662070773737725018)
XLA Ops:
  11.6 22.5 %all_to_all.70 = bf16[16,12,2048]{2,1,0:T(8,128)(2,1)} all-to-all(bf16[16,12,2048]{2,1,0:T(8,128)(2,1)S(1)} %bitcast.270), channel_id=1, replica_groups=mesh['section'=4,'expert'=16,'dp'=4] {'expert'}, dimensions={0} | all-to-all | bytes 1572864 | tf_op jit(solution)/shard_map/all_to_all | solution.py:56
  36.3 3.0 fusion.40
  46.2 4.3 all-to-all-start.1
  50.6 14.9 %all-to-all-done.1 = bf16[16,12,2048]{2,1,0:T(8,128)(2,1)} async-done(((bf16[16,12,2048]{2,1,0:T(8,128)(2,1)}), bf16[16,12,2048]{2,1,0:T(8,128)(2,1)}, u32[]{:S(2)}, u32[]{:S(2)}) %all-to-all-start.1) | async-done | bytes 786464 | tf_op jit(solution)/shard_map/all_to_all | solution.py:65
  65.5 2.4 fusion.63
  68.0 51.2 %all-reduce.8.cloned.1.call-done = bf16[32,2048]{1,0:T(8,128)(2,1)} async-done(((bf16[32,2048]{1,0:T(8,128)(2,1)}), bf16[32,2048]{1,0:T(8,128)(2,1)}) %all-reduce.8.cloned.1.call-update) | async-done | bytes 131088 | tf_op jit(solution)/shard_map/psum | solution.py:69
  121.6 5.5 collective-permute-done
  128.6 22.0 %all_to_all.71 = bf16[16,12,2048]{2,1,0:T(8,128)(2,1)} all-to-all(bf16[16,12,2048]{2,1,0:T(8,128)(2,1)S(1)} %bitcast.271), channel_id=1, replica_groups=mesh['section'=4,'expert'=16,'dp'=4] {'expert'}, dimensions={0} | all-to-all | bytes 1572864 | tf_op jit(solution)/shard_map/all_to_all | solution.py:56
  152.7 3.0 fusion.38
  162.6 4.3 all-to-all-start.3
  167.0 14.6 %all-to-all-done.3 = bf16[16,12,2048]{2,1,0:T(8,128)(2,1)} async-done(((bf16[16,12,2048]{2,1,0:T(8,128)(2,1)}), bf16[16,12,2048]{2,1,0:T(8,128)(2,1)}, u32[]{:S(2)}, u32[]{:S(2)}) %all-to-all-start.3) | async-done | bytes 786464 | tf_op jit(solution)/shard_map/all_to_all | solution.py:65
  181.6 2.4 fusion.64
  185.0 48.1 %all-reduce.10.cloned.1.call-done = bf16[32,2048]{1,0:T(8,128)(2,1)} async-done(((bf16[32,2048]{1,0:T(8,128)(2,1)}), bf16[32,2048]{1,0:T(8,128)(2,1)}) %all-reduce.10.cloned.1.call-update) | async-done | bytes 131088 | tf_op jit(solution)/shard_map/psum | solution.py:69
  236.0 5.5 collective-permute-done.1
  243.0 22.0 %all_to_all.72 = bf16[16,12,2048]{2,1,0:T(8,128)(2,1)} all-to-all(bf16[16,12,2048]{2,1,0:T(8,128)(2,1)S(1)} %bitcast.272), channel_id=1, replica_groups=mesh['section'=4,'expert'=16,'dp'=4] {'expert'}, dimensions={0} | all-to-all | bytes 1572864 | tf_op jit(solution)/shard_map/all_to_all | solution.py:56
  267.1 3.0 fusion.36
  276.9 4.3 all-to-all-start.5
  281.4 14.5 %all-to-all-done.5 = bf16[16,12,2048]{2,1,0:T(8,128)(2,1)} async-done(((bf16[16,12,2048]{2,1,0:T(8,128)(2,1)}), bf16[16,12,2048]{2,1,0:T(8,128)(2,1)}, u32[]{:S(2)}, u32[]{:S(2)}) %all-to-all-start.5) | async-done | bytes 786464 | tf_op jit(solution)/shard_map/all_to_all | solution.py:65
  295.9 2.4 fusion.65
  299.3 48.1 %all-reduce.12.cloned.1.call-done = bf16[32,2048]{1,0:T(8,128)(2,1)} async-done(((bf16[32,2048]{1,0:T(8,128)(2,1)}), bf16[32,2048]{1,0:T(8,128)(2,1)}) %all-reduce.12.cloned.1.call-update) | async-done | bytes 131088 | tf_op jit(solution)/shard_map/psum | solution.py:69
  350.3 5.5 collective-permute-done.2
  357.3 22.0 %all_to_all.73 = bf16[16,12,2048]{2,1,0:T(8,128)(2,1)} all-to-all(bf16[16,12,2048]{2,1,0:T(8,128)(2,1)S(1)} %bitcast.273), channel_id=1, replica_groups=mesh['section'=4,'expert'=16,'dp'=4] {'expert'}, dimensions={0} | all-to-all | bytes 1572864 | tf_op jit(solution)/shard_map/all_to_all | solution.py:56
  381.4 3.0 fusion.34
  391.3 4.3 all-to-all-start.7
  395.7 14.6 %all-to-all-done.7 = bf16[16,12,2048]{2,1,0:T(8,128)(2,1)} async-done(((bf16[16,12,2048]{2,1,0:T(8,128)(2,1)}), bf16[16,12,2048]{2,1,0:T(8,128)(2,1)}, u32[]{:S(2)}, u32[]{:S(2)}) %all-to-all-start.7) | async-done | bytes 786464 | tf_op jit(solution)/shard_map/all_to_all | solution.py:65
  410.3 2.4 fusion.66
  413.7 48.1 %all-reduce.14.cloned.1.call-done = bf16[32,2048]{1,0:T(8,128)(2,1)} async-done(((bf16[32,2048]{1,0:T(8,128)(2,1)}), bf16[32,2048]{1,0:T(8,128)(2,1)}) %all-reduce.14.cloned.1.call-update) | async-done | bytes 131088 | tf_op jit(solution)/shard_map/psum | solution.py:69
  464.7 5.5 collective-permute-done.3
  471.7 22.0 %all_to_all.74 = bf16[16,12,2048]{2,1,0:T(8,128)(2,1)} all-to-all(bf16[16,12,2048]{2,1,0:T(8,128)(2,1)S(1)} %bitcast.274), channel_id=1, replica_groups=mesh['section'=4,'expert'=16,'dp'=4] {'expert'}, dimensions={0} | all-to-all | bytes 1572864 | tf_op jit(solution)/shard_map/all_to_all | solution.py:56
  495.8 3.0 fusion.32
  505.6 4.3 all-to-all-start.9
  510.3 14.3 %all-to-all-done.9 = bf16[16,12,2048]{2,1,0:T(8,128)(2,1)} async-done(((bf16[16,12,2048]{2,1,0:T(8,128)(2,1)}), bf16[16,12,2048]{2,1,0:T(8,128)(2,1)}, u32[]{:S(2)}, u32[]{:S(2)}) %all-to-all-start.9) | async-done | bytes 786464 | tf_op jit(solution)/shard_map/all_to_all | solution.py:65
  524.7 2.4 fusion.67
  528.0 48.1 %all-reduce.16.cloned.1.call-done = bf16[32,2048]{1,0:T(8,128)(2,1)} async-done(((bf16[32,2048]{1,0:T(8,128)(2,1)}), bf16[32,2048]{1,0:T(8,128)(2,1)}) %all-reduce.16.cloned.1.call-update) | async-done | bytes 131088 | tf_op jit(solution)/shard_map/psum | solution.py:69
  579.1 5.5 collective-permute-done.4
  586.1 22.0 %all_to_all.75 = bf16[16,12,2048]{2,1,0:T(8,128)(2,1)} all-to-all(bf16[16,12,2048]{2,1,0:T(8,128)(2,1)S(1)} %bitcast.275), channel_id=1, replica_groups=mesh['section'=4,'expert'=16,'dp'=4] {'expert'}, dimensions={0} | all-to-all | bytes 1572864 | tf_op jit(solution)/shard_map/all_to_all | solution.py:56
  610.2 3.1 fusion.30
  620.0 4.3 all-to-all-start.11
  624.4 14.6 %all-to-all-done.11 = bf16[16,12,2048]{2,1,0:T(8,128)(2,1)} async-done(((bf16[16,12,2048]{2,1,0:T(8,128)(2,1)}), bf16[16,12,2048]{2,1,0:T(8,128)(2,1)}, u32[]{:S(2)}, u32[]{:S(2)}) %all-to-all-start.11) | async-done | bytes 786464 | tf_op jit(solution)/shard_map/all_to_all | solution.py:65
  639.0 2.4 fusion.68
  642.4 48.1 %all-reduce.18.cloned.1.call-done = bf16[32,2048]{1,0:T(8,128)(2,1)} async-done(((bf16[32,2048]{1,0:T(8,128)(2,1)}), bf16[32,2048]{1,0:T(8,128)(2,1)}) %all-reduce.18.cloned.1.call-update) | async-done | bytes 131088 | tf_op jit(solution)/shard_map/psum | solution.py:69
  693.4 5.5 collective-permute-done.5
  700.4 22.0 %all_to_all.76 = bf16[16,12,2048]{2,1,0:T(8,128)(2,1)} all-to-all(bf16[16,12,2048]{2,1,0:T(8,128)(2,1)S(1)} %bitcast.276), channel_id=1, replica_groups=mesh['section'=4,'expert'=16,'dp'=4] {'expert'}, dimensions={0} | all-to-all | bytes 1572864 | tf_op jit(solution)/shard_map/all_to_all | solution.py:56
  724.5 3.0 fusion.28
  734.4 4.3 all-to-all-start.13
  738.8 14.6 %all-to-all-done.13 = bf16[16,12,2048]{2,1,0:T(8,128)(2,1)} async-done(((bf16[16,12,2048]{2,1,0:T(8,128)(2,1)}), bf16[16,12,2048]{2,1,0:T(8,128)(2,1)}, u32[]{:S(2)}, u32[]{:S(2)}) %all-to-all-start.13) | async-done | bytes 786464 | tf_op jit(solution)/shard_map/all_to_all | solution.py:65
  753.4 2.4 fusion.69
  756.7 48.1 %all-reduce.20.cloned.1.call-done = bf16[32,2048]{1,0:T(8,128)(2,1)} async-done(((bf16[32,2048]{1,0:T(8,128)(2,1)}), bf16[32,2048]{1,0:T(8,128)(2,1)}) %all-reduce.20.cloned.1.call-update) | async-done | bytes 131088 | tf_op jit(solution)/shard_map/psum | solution.py:69
  (165 shorter events, 101.1 us)
Async XLA Ops:
  6.5 36.4 %copy-start = (bf16[1,768,2048]{2,1,0:T(8,128)(2,1)S(1)}, bf16[1,768,2048]{2,1,0:T(8,128)(2,1)}, u32[]{:S(2)}) copy-start(bf16[1,768,2048]{2,1,0:T(8,128)(2,1)} %param.10) | copy-start | bytes 9437188
  36.3 3.1 copy-start.2
  36.3 3.3 copy-start.9
  46.2 19.3 %all-to-all-start.1 = ((bf16[16,12,2048]{2,1,0:T(8,128)(2,1)}), bf16[16,12,2048]{2,1,0:T(8,128)(2,1)}, u32[]{:S(2)}, u32[]{:S(2)}) async-start(bf16[16,12,2048]{2,1,0:T(8,128)(2,1)} %copy.23), calls=%async_computation.1 | async-start | bytes 2097152 | tf_op jit(solution)/shard_map/all_to_all | solution.py:65
  50.5 68.7 %all-reduce.8.cloned.1.call-start = ((), (), s32[]{:S(2)}) async-start(), calls=%async_computation.14 | async-start | bytes 262144 | tf_op jit(solution)/shard_map/psum | solution.py:69
  120.3 7.9 copy-start.1
  120.3 6.8 collective-permute-start
  152.7 3.1 copy-start.3
  152.7 3.3 copy-start.10
  162.6 19.0 %all-to-all-start.3 = ((bf16[16,12,2048]{2,1,0:T(8,128)(2,1)}), bf16[16,12,2048]{2,1,0:T(8,128)(2,1)}, u32[]{:S(2)}, u32[]{:S(2)}) async-start(bf16[16,12,2048]{2,1,0:T(8,128)(2,1)} %copy.27), calls=%async_computation.3 | async-start | bytes 2097152 | tf_op jit(solution)/shard_map/all_to_all | solution.py:65
  166.9 66.1 %all-reduce.10.cloned.1.call-start = ((), (), s32[]{:S(2)}) async-start(), calls=%async_computation.15 | async-start | bytes 262144 | tf_op jit(solution)/shard_map/psum | solution.py:69
  234.7 6.8 collective-permute-start.1
  267.0 3.1 copy-start.4
  267.0 3.3 copy-start.11
  276.9 19.0 %all-to-all-start.5 = ((bf16[16,12,2048]{2,1,0:T(8,128)(2,1)}), bf16[16,12,2048]{2,1,0:T(8,128)(2,1)}, u32[]{:S(2)}, u32[]{:S(2)}) async-start(bf16[16,12,2048]{2,1,0:T(8,128)(2,1)} %copy.31), calls=%async_computation.5 | async-start | bytes 2097152 | tf_op jit(solution)/shard_map/all_to_all | solution.py:65
  281.3 66.2 %all-reduce.12.cloned.1.call-start = ((), (), s32[]{:S(2)}) async-start(), calls=%async_computation.16 | async-start | bytes 262144 | tf_op jit(solution)/shard_map/psum | solution.py:69
  349.0 6.8 collective-permute-start.2
  381.4 3.1 copy-start.5
  381.4 3.3 copy-start.12
  391.3 19.0 %all-to-all-start.7 = ((bf16[16,12,2048]{2,1,0:T(8,128)(2,1)}), bf16[16,12,2048]{2,1,0:T(8,128)(2,1)}, u32[]{:S(2)}, u32[]{:S(2)}) async-start(bf16[16,12,2048]{2,1,0:T(8,128)(2,1)} %copy.35), calls=%async_computation.7 | async-start | bytes 2097152 | tf_op jit(solution)/shard_map/all_to_all | solution.py:65
  395.6 66.2 %all-reduce.14.cloned.1.call-start = ((), (), s32[]{:S(2)}) async-start(), calls=%async_computation.17 | async-start | bytes 262144 | tf_op jit(solution)/shard_map/psum | solution.py:69
  463.4 6.8 collective-permute-start.3
  495.8 3.1 copy-start.6
  495.8 3.3 copy-start.13
  505.6 19.0 %all-to-all-start.9 = ((bf16[16,12,2048]{2,1,0:T(8,128)(2,1)}), bf16[16,12,2048]{2,1,0:T(8,128)(2,1)}, u32[]{:S(2)}, u32[]{:S(2)}) async-start(bf16[16,12,2048]{2,1,0:T(8,128)(2,1)} %copy.39), calls=%async_computation.9 | async-start | bytes 2097152 | tf_op jit(solution)/shard_map/all_to_all | solution.py:65
  510.0 66.2 %all-reduce.16.cloned.1.call-start = ((), (), s32[]{:S(2)}) async-start(), calls=%async_computation.18 | async-start | bytes 262144 | tf_op jit(solution)/shard_map/psum | solution.py:69
  577.8 6.8 collective-permute-start.4
  610.2 3.1 copy-start.7
  610.2 3.3 copy-start.14
  620.0 19.0 %all-to-all-start.11 = ((bf16[16,12,2048]{2,1,0:T(8,128)(2,1)}), bf16[16,12,2048]{2,1,0:T(8,128)(2,1)}, u32[]{:S(2)}, u32[]{:S(2)}) async-start(bf16[16,12,2048]{2,1,0:T(8,128)(2,1)} %copy.43), calls=%async_computation.11 | async-start | bytes 2097152 | tf_op jit(solution)/shard_map/all_to_all | solution.py:65
  624.4 66.1 %all-reduce.18.cloned.1.call-start = ((), (), s32[]{:S(2)}) async-start(), calls=%async_computation.19 | async-start | bytes 262144 | tf_op jit(solution)/shard_map/psum | solution.py:69
  692.1 6.8 collective-permute-start.5
  724.5 3.1 copy-start.8
  724.5 3.3 copy-start.15
  734.4 19.0 %all-to-all-start.13 = ((bf16[16,12,2048]{2,1,0:T(8,128)(2,1)}), bf16[16,12,2048]{2,1,0:T(8,128)(2,1)}, u32[]{:S(2)}, u32[]{:S(2)}) async-start(bf16[16,12,2048]{2,1,0:T(8,128)(2,1)} %copy.47), calls=%async_computation.13 | async-start | bytes 2097152 | tf_op jit(solution)/shard_map/all_to_all | solution.py:65
  738.7 66.2 %all-reduce.20.cloned.1.call-start = ((), (), s32[]{:S(2)}) async-start(), calls=%async_computation.20 | async-start | bytes 262144 | tf_op jit(solution)/shard_map/psum | solution.py:69
Sparse Core Ops, SparseCore 0:
  68.1 51.0 all-reduce.7
  184.2 48.8 all-reduce.9
  298.5 48.8 all-reduce.11
  412.9 48.8 all-reduce.13
  527.2 48.8 all-reduce.15
  641.6 48.8 all-reduce.17
  755.9 48.8 all-reduce.19
where the time goes:
time: 820 us; the launch traced here: 813 us
  waiting for transfers between devices  475 us (58%)
  blocking collectives  154 us (19%)
  matrix products  65.3 us (8%)
  local copies, waits for them, and re-layouts  46.7 us (6%)
  starting transfers between devices  38.6 us (5%)
  other arithmetic  19 us (2%)
  between operations  14.2 us (2%)
    psum x7, waiting for transfers between devices, shards(): update = lax.psum(local_sum.astype(jnp.bfloat16), 'dp').astype(jnp.float32)  340 us
    all_to_all x7, blocking collectives, shards(): lax.all_to_all(outgoing, 'expert', split_axis=0, concat_axis=0, tiled=True)  154 us
    all_to_all x7, waiting for transfers between devices, shards(): lax.all_to_all(rounded, 'expert', split_axis=0, concat_axis=0, tiled=True)  102 us
    ppermute x6, waiting for transfers between devices, from_behind(): lax.ppermute(value, axis, [(source, source + steps) for source in range(i...  33.1 us
    all_to_all x7, starting transfers between devices, shards(): lax.all_to_all(rounded, 'expert', split_axis=0, concat_axis=0, tiled=True)  30.4 us
    dot_general x7, matrix products, shards(): gate = jnp.dot(rows, w_gate, preferred_element_type=jnp.float32)  21.3 us
    dot_general x7, matrix products, shards(): jnp.einsum('jct,jcd->td', place_all, returned, preferred_element_type=jnp...  17 us
  transfers between devices with their start and end apart: 20, of which 20 were waited for; matrix products, arithmetic and copies ran while one was open for 1% of the time, Pallas kernels for 0%

commit v1 on v0

v1 whole, which is shorter than its diff:
```python
import functools

import jax
import jax.numpy as jnp
import numpy as np
from jax import lax
from jax.experimental import pallas as pl
from jax.experimental.pallas import tpu as pltpu
from jax.sharding import PartitionSpec as P

MESH = pl.DeviceIdType.MESH
EXPERTS = 4
CHUNKS = 4
F32 = jnp.float32
BF16 = jnp.bfloat16


def dist(shift, size):
    return min(shift, size - shift)


def wait_bytes(ref, sem):
    pltpu.make_async_copy(ref, ref, sem).wait()


def kernel(
    n_section,
    split,
    cap,
    x_ref,
    ids_ref,
    gain_ref,
    tgt_col_ref,
    tgt_row_ref,
    perm_ref,
    perm_t_ref,
    wg_hbm,
    wu_hbm,
    wd_hbm,
    out_ref,
    wg,
    wu,
    wd,
    gain,
    place,
    place_t,
    hbuf,
    dsend,
    drecv,
    dother,
    rows,
    act,
    csend,
    crecv,
    own,
    packed,
    rsend,
    rrecv,
    hsend,
    hrecv,
    zrecv,
    ostage,
    obuf,
    wsem,
    dsend_sem,
    drecv_sem,
    fsend_sem,
    frecv_sem,
    csend_sem,
    crecv_sem,
    rsend_sem,
    rrecv_sem,
    hsend_sem,
    hrecv_sem,
    zsend_sem,
    zrecv_sem,
    osend_sem,
    orecv_sem,
):
    spans, tok, width = x_ref.shape
    half = width // 2
    chunk = half // CHUNKS
    hidden = wg.shape[1]
    group = split * cap
    last = n_section - 1
    s = lax.axis_index("section")
    me = lax.axis_index("expert")
    d = lax.axis_index("dp")
    core, zh = d % 2, d // 2
    ex, ey = me // split, me % split
    other = {"dp": zh * 2 + 1 - core}
    across = {"dp": (1 - zh) * 2 + core}

    mine = pl.ds(pl.multiple_of(core * half, half), half)
    theirs = pl.ds(pl.multiple_of((1 - core) * half, half), half)
    low, high = pl.ds(0, half), pl.ds(half, half)
    loads = []
    for side, (source, target) in enumerate(((mine, low), (theirs, high))):
        loads.append((wg_hbm.at[0, source], wg.at[target]))
        loads.append((wu_hbm.at[0, source], wu.at[target]))
        loads.append((wd_hbm.at[0, :, source], wd.at[side]))
    loads = [
        pltpu.make_async_copy(source, target, wsem.at[i])
        for i, (source, target) in enumerate(loads)
    ]
    for load in loads:
        load.start()

    shifts = sorted(
        ((jx, jy) for jx in range(EXPERTS) for jy in range(split) if jx or jy),
        key=lambda j: -dist(j[0], EXPERTS) - dist(j[1], split),
    )

    def peer(jx, jy):
        return {"expert": ((ex + jx) % EXPERTS) * split + (ey + jy) % split}

    barrier = pltpu.get_barrier_semaphore()

    def greet(device):
        pl.semaphore_signal(barrier, inc=1, device_id=device, device_id_type=MESH)

    def section_peers(section):
        return [
            {"section": section, "dp": zh * 2 + core},
            {"section": section, "dp": zh * 2 + 1 - core},
            {"section": section, "dp": (1 - zh) * 2 + core},
        ]

    for jx, jy in shifts:
        greet(peer(jx, jy))
    greet(other)
    greet(across)

    @pl.when(s < last)
    def _():
        for device in section_peers(s + 1):
            greet(device)

    @pl.when(s > 0)
    def _():
        for device in section_peers(s - 1):
            greet(device)

    gain[0] = gain_ref[:, mine].astype(F32)
    gain[1] = gain_ref[:, theirs].astype(F32)

    def placement(c, carry):
        n = CHUNKS * tok
        row = lax.broadcasted_iota(jnp.int32, (n, n), 0)
        col = lax.broadcasted_iota(jnp.int32, (n, n), 1)
        ids_col = ids_ref[c]
        ids_row = jnp.sum(jnp.where(row == col, ids_col, 0), axis=0, keepdims=True)
        same = (ids_col == ids_row) & (row // tok == col // tok)
        rank_row = jnp.sum((same & (row < col)).astype(jnp.int32), axis=0, keepdims=True)
        rank_col = jnp.sum((same & (col < row)).astype(jnp.int32), axis=1, keepdims=True)
        stride = EXPERTS * cap
        key_row = ids_row * cap + rank_row + stride * (col[0:1] // tok)
        key_col = ids_col * cap + rank_col + stride * (row[:, 0:1] // tok)
        place[c] = (tgt_col_ref[...] == key_row).astype(F32).astype(BF16)
        place_t[c] = (tgt_row_ref[...] == key_col).astype(F32).astype(BF16)
        return carry

    lax.fori_loop(0, spans, placement, 0)

    expected = len(shifts) + 2 + 3 * (s < last).astype(jnp.int32) + 3 * (s > 0).astype(jnp.int32)
    pl.semaphore_wait(barrier, expected)

    def remote(source, target, send_sem, recv_sem, device):
        pltpu.make_async_remote_copy(
            src_ref=source,
            dst_ref=target,
            send_sem=send_sem,
            recv_sem=recv_sem,
            device_id=device,
            device_id_type=MESH,
        ).start()

    def dispatch(c):
        @pl.when(s == 0)
        def _():
            for q in range(CHUNKS):
                cols = pl.ds(pl.multiple_of(core * half + q * chunk, chunk), chunk)
                hbuf[c, q * tok : (q + 1) * tok] = x_ref[c, :, cols]

        @pl.when(s > 0)
        def _():
            wait_bytes(hrecv.at[c], hrecv_sem.at[c])
            hbuf[c] = (hrecv[c, 0].astype(F32) + hrecv[c, 1].astype(F32)).astype(BF16)

        sent = jnp.dot(place[c], hbuf[c], preferred_element_type=F32).astype(BF16)
        dsend[c] = sent.reshape(EXPERTS, CHUNKS * cap, chunk)
        for jx, jy in shifts:
            ix, iy = (-jx) % EXPERTS, (-jy) % split
            remote(
                dsend.at[c, (ex + jx) % EXPERTS],
                drecv.at[c, ix, iy],
                dsend_sem.at[c],
                drecv_sem.at[c, ix],
                peer(jx, jy),
            )
        pltpu.make_async_copy(dsend.at[c, ex], drecv.at[c, 0, 0], drecv_sem.at[c, 0]).start()

        @pl.when(s > 0)
        def _():
            for q in range(CHUNKS):
                ostage[c, :, q * chunk : (q + 1) * chunk] = hbuf[c, q * tok : (q + 1) * tok]
            for k in range(2):
                remote(
                    ostage.at[c],
                    obuf.at[c, core],
                    osend_sem.at[c],
                    orecv_sem.at[c],
                    {"section": s - 1, "dp": zh * 2 + k},
                )

    def unpack(source, i, side):
        z = jnp.dot(
            perm_ref[...], source.reshape(split * CHUNKS * cap, chunk), preferred_element_type=F32
        )
        total = jnp.zeros((group, 1), F32)
        for q in range(CHUNKS):
            part = z[q * group : (q + 1) * group]
            cols = slice(q * chunk, (q + 1) * chunk)
            place_at = slice(side * half + q * chunk, side * half + (q + 1) * chunk)
            rows[i * group : (i + 1) * group, place_at] = (part * gain[side, :, cols]).astype(BF16)
            total = total + jnp.sum(part * part, axis=1, keepdims=True)
        return total

    nearest = sorted(range(EXPERTS), key=lambda i: dist(i, EXPERTS))

    def experts(c):
        squares = [None] * EXPERTS
        for i in nearest:
            wait_bytes(drecv.at[c, i], drecv_sem.at[c, i])
            remote(drecv.at[c, i], dother.at[c, i], fsend_sem.at[c], frecv_sem.at[c, i], other)
            squares[i] = unpack(drecv[c, i], i, 0)
        for i in nearest:
            wait_bytes(dother.at[c, i], frecv_sem.at[c, i])
            squares[i] = squares[i] + unpack(dother[c, i], i, 1)
        scale = lax.rsqrt(jnp.concatenate(squares, axis=0) / width + 1e-5)
        for j in range(hidden // 256):
            cols = slice(j * 256, (j + 1) * 256)
            gate = jnp.dot(rows[...], wg[:, cols], preferred_element_type=F32) * scale
            upper = jnp.dot(rows[...], wu[:, cols], preferred_element_type=F32) * scale
            act[:, cols] = (gate / (1.0 + jnp.exp(-gate)) * upper).astype(BF16)
        for q in range(CHUNKS):
            cols = slice(q * chunk, (q + 1) * chunk)
            csend[c, q] = jnp.dot(act[...], wd[1, :, cols], preferred_element_type=F32).astype(BF16)
            remote(csend.at[c, q], crecv.at[c, q], csend_sem.at[c], crecv_sem.at[c, q], other)
        for q in range(CHUNKS):
            cols = slice(q * chunk, (q + 1) * chunk)
            own[q] = jnp.dot(act[...], wd[0, :, cols], preferred_element_type=F32)
        for q in range(CHUNKS):
            wait_bytes(crecv.at[c, q], crecv_sem.at[c, q])
            both = (own[q] + crecv[c, q].astype(F32)).astype(BF16)
            for i in range(EXPERTS):
                packed[i, q] = both[i * group : (i + 1) * group]
        for i in reversed(nearest):
            out = jnp.dot(
                perm_t_ref[...],
                packed[i].reshape(CHUNKS * group, chunk),
                preferred_element_type=F32,
            ).astype(BF16)
            rsend[c, i] = out.reshape(split, CHUNKS * cap, chunk)
            for jx, jy in shifts:
                if jx == i:
                    iy = (-jy) % split
                    remote(
                        rsend.at[c, jx, jy],
                        rrecv.at[c, ex, iy],
                        rsend_sem.at[c],
                        rrecv_sem.at[c],
                        peer(jx, jy),
                    )
        pltpu.make_async_copy(rsend.at[c, 0, 0], rrecv.at[c, ex, 0], rrecv_sem.at[c]).start()

    def combine(c):
        wait_bytes(rrecv.at[c], rrecv_sem.at[c])
        back = rrecv[c].reshape(EXPERTS * split * CHUNKS * cap, chunk)
        update = jnp.dot(place_t[c], back, preferred_element_type=F32)
        base = hbuf[c].astype(F32) * (zh == 0).astype(F32)
        hsend[c] = (base + update).astype(BF16)

        @pl.when(s < last)
        def _():
            for k in range(2):
                remote(
                    hsend.at[c],
                    hrecv.at[c, zh],
                    hsend_sem.at[c],
                    hrecv_sem.at[c],
                    {"section": s + 1, "dp": k * 2 + core},
                )

        @pl.when(s == last)
        def _():
            remote(hsend.at[c], zrecv.at[c], zsend_sem.at[c], zrecv_sem.at[c], across)

    def finish(c):
        wait_bytes(zrecv.at[c], zrecv_sem.at[c])
        whole = (hsend[c].astype(F32) + zrecv[c].astype(F32)).astype(BF16)
        for q in range(CHUNKS):
            obuf[c, core, :, q * chunk : (q + 1) * chunk] = whole[q * tok : (q + 1) * tok]
        remote(obuf.at[c, core], obuf.at[c, core], osend_sem.at[c], orecv_sem.at[c], other)

    def tick(t, carry):
        @pl.when(t < spans)
        def _():
            dispatch(t)

        @pl.when(t == 1)
        def _():
            for load in loads:
                load.wait()

        @pl.when((t >= 1) & (t < spans + 1))
        def _():
            experts(t - 1)

        @pl.when((t >= 2) & (t < spans + 2))
        def _():
            combine(t - 2)

        @pl.when((t >= 3) & (s == last))
        def _():
            finish(t - 3)

        return carry

    lax.fori_loop(0, spans + 3, tick, 0)

    def drain(c, carry):
        everyone = pl.ds(0, split - 1)
        wait_bytes(drecv.at[c, pl.ds(0, EXPERTS - 1)], dsend_sem.at[c])
        wait_bytes(drecv.at[c, EXPERTS - 1, everyone], dsend_sem.at[c])
        wait_bytes(drecv.at[c, pl.ds(0, EXPERTS - 1)], rsend_sem.at[c])
        wait_bytes(drecv.at[c, EXPERTS - 1, everyone], rsend_sem.at[c])
        wait_bytes(drecv.at[c], fsend_sem.at[c])
        wait_bytes(csend.at[c], csend_sem.at[c])

        @pl.when(s < last)
        def _():
            wait_bytes(hrecv.at[c], hsend_sem.at[c])
            wait_bytes(obuf.at[c], orecv_sem.at[c])

        @pl.when(s == last)
        def _():
            wait_bytes(hsend.at[c], zsend_sem.at[c])
            wait_bytes(ostage.at[c], osend_sem.at[c])
            wait_bytes(ostage.at[c], orecv_sem.at[c])

        @pl.when(s > 0)
        def _():
            wait_bytes(obuf.at[c], osend_sem.at[c])

        out_ref[0, c, :, 0:half] = obuf[c, 0]
        out_ref[0, c, :, half:width] = obuf[c, 1]
        return carry

    lax.fori_loop(0, spans, drain, 0)


def shards(inputs, norm_gain, gate_weight, up_weight, down_weight, expert_ids):
    n_section = lax.axis_size("section")
    n_expert = lax.axis_size("expert")
    split = n_expert // EXPERTS
    spans, tok, width = inputs.shape
    hidden = gate_weight.shape[-1]
    cap = tok // EXPERTS * 3 // 2
    half = width // 2
    chunk = half // CHUNKS
    group = split * cap
    total = EXPERTS * group
    block = CHUNKS * cap

    stride = EXPERTS * cap
    e, q, r = np.meshgrid(np.arange(EXPERTS), np.arange(CHUNKS), np.arange(cap), indexing="ij")
    key = (e * cap + r + stride * q).reshape(EXPERTS, block)
    tgt_col = key.reshape(-1, 1).astype(np.int32)
    tgt_row = np.repeat(key[:, None], split, axis=1).reshape(1, -1).astype(np.int32)
    order = np.arange(split * block).reshape(split, CHUNKS, cap).transpose(1, 0, 2).reshape(-1)
    perm = np.eye(split * block, dtype=np.float32)[order]
    ids = jnp.tile(expert_ids[0], (1, CHUNKS, 1))

    vmem = pl.BlockSpec(memory_space=pltpu.VMEM)
    hbm = pl.BlockSpec(memory_space=pl.ANY)
    dma = pltpu.SemaphoreType.DMA
    blocks = (spans, EXPERTS, split, block, chunk)
    return pl.pallas_call(
        functools.partial(kernel, n_section, split, cap),
        out_shape=jax.ShapeDtypeStruct((1, spans, tok, width), BF16),
        in_specs=[vmem] * 7 + [hbm] * 3,
        out_specs=vmem,
        scratch_shapes=[
            pltpu.VMEM((width, hidden), BF16),
            pltpu.VMEM((width, hidden), BF16),
            pltpu.VMEM((2, hidden, half), BF16),
            pltpu.VMEM((2, 1, half), F32),
            pltpu.VMEM((spans, EXPERTS * block, CHUNKS * tok), BF16),
            pltpu.VMEM((spans, CHUNKS * tok, EXPERTS * split * block), BF16),
            pltpu.VMEM((spans, CHUNKS * tok, chunk), BF16),
            pltpu.VMEM((spans, EXPERTS, block, chunk), BF16),
            pltpu.VMEM(blocks, BF16),
            pltpu.VMEM(blocks, BF16),
            pltpu.VMEM((total, width), BF16),
            pltpu.VMEM((total, hidden), BF16),
            pltpu.VMEM((spans, CHUNKS, total, chunk), BF16),
            pltpu.VMEM((spans, CHUNKS, total, chunk), BF16),
            pltpu.VMEM((CHUNKS, total, chunk), F32),
            pltpu.VMEM((EXPERTS, CHUNKS, group, chunk), BF16),
            pltpu.VMEM(blocks, BF16),
            pltpu.VMEM(blocks, BF16),
            pltpu.VMEM((spans, CHUNKS * tok, chunk), BF16),
            pltpu.VMEM((spans, 2, CHUNKS * tok, chunk), BF16),
            pltpu.VMEM((spans, CHUNKS * tok, chunk), BF16),
            pltpu.VMEM((spans, tok, half), BF16),
            pltpu.VMEM((spans, 2, tok, half), BF16),
            dma((6,)),
            dma((spans,)),
            dma((spans, EXPERTS)),
            dma((spans,)),
            dma((spans, EXPERTS)),
            dma((spans,)),
            dma((spans, CHUNKS)),
            dma((spans,)),
            dma((spans,)),
            dma((spans,)),
            dma((spans,)),
            dma((spans,)),
            dma((spans,)),
            dma((spans,)),
            dma((spans,)),
        ],
        compiler_params=pltpu.CompilerParams(
            collective_id=0, has_side_effects=True, vmem_limit_bytes=56 * 2**20
        ),
        name="layers",
    )(
        inputs,
        ids,
        norm_gain,
        jnp.asarray(tgt_col),
        jnp.asarray(tgt_row),
        jnp.asarray(perm, BF16),
        jnp.asarray(perm.T, BF16),
        gate_weight,
        up_weight,
        down_weight,
    )


def solution(mesh):
    placed = (
        P(None, "expert", None),
        P("section", None),
        P("section", None, ("expert", "dp")),
        P("section", None, ("expert", "dp")),
        P("section", ("expert", "dp"), None),
        P("section", None, "expert", None),
    )
    return jax.shard_map(
        shards,
        mesh=mesh,
        in_specs=placed,
        out_specs=P("section", None, "expert", None),
        check_vma=False,
    )
```

time: 820 us -> 160 us (0.20)
  waiting for transfers between devices: 475 us -> 0 us
  Pallas kernels: 0 us -> 156 us
  blocking collectives: 154 us -> 0 us
  matrix products: 65.3 us -> 0 us
  local copies, waits for them, and re-layouts: 46.7 us -> 3.54 us
  starting transfers between devices: 38.6 us -> 0 us
  other arithmetic: 19 us -> 0 us
  between operations: 14.2 us -> 0.01 us
    psum x7 -> x0, waiting for transfers between devices: 340 us -> none  [shards(): update = lax.psum(local_sum.astype(jnp.bfloat16), 'dp').astype(jnp.float32)]
    pallas_call x0 -> x1, Pallas kernels: none -> 156 us  [shards(): pl.pallas_call(functools.partial(kernel, n_section, split, cap), out_shap...]
    all_to_all x7 -> x0, blocking collectives: 154 us -> none  [shards(): lax.all_to_all(outgoing, 'expert', split_axis=0, concat_axis=0, tiled=True)]
    all_to_all x7 -> x0, waiting for transfers between devices: 102 us -> none  [shards(): lax.all_to_all(rounded, 'expert', split_axis=0, concat_axis=0, tiled=True)]
    dot_general x42 -> x0, matrix products: 65.3 us -> none  [the longest x7 21.3 us: shards(): gate = jnp.dot(rows, w_gate, preferred_element_type=jnp.float32)]
    ppermute x6 -> x0, waiting for transfers between devices: 33.1 us -> none  [from_behind(): lax.ppermute(value, axis, [(source, source + steps) for source in range(i...]
    all_to_all x7 -> x0, starting transfers between devices: 30.4 us -> none  [shards(): lax.all_to_all(rounded, 'expert', split_axis=0, concat_axis=0, tiled=True)]
    reshape x7 -> x0, local copies, waits for them, and re-layouts: 14.9 us -> none  [shards(): rows = arrived.reshape(n_expert * capacity, width)]
  transfers between devices with their start and end apart: 20 -> 0, of which waited for: 20 -> 0; matrix products, arithmetic and copies ran while one was open for 1% -> 0% of each run, Pallas kernels for 0% -> 0%
where the time goes in v1:
time: 160 us
  Pallas kernels  156 us (98%)
  local copies, waits for them, and re-layouts  3.54 us (2%)
    pallas_call x1, Pallas kernels, shards(): pl.pallas_call(functools.partial(kernel, n_section, split, cap), out_shap...  156 us

profile of v1, /device:TPU:97, one launch (start us, length us, event | category | flops | bytes accessed | tf_op | source)
XLA Modules:
  0.0 160.0 jit_solution(1731914928761150758)
XLA Ops:
  0.0 0.7 tile.11
  0.7 1.0 tile.13.ids_ref
  1.7 156.4 %layers.1 = bf16[1,4,32,2048]{3,2,1,0:T(8,128)(2,1)} custom-call(bf16[4,32,2048]{2,1,0:T(8,128)(2,1)} %x_ref.1, s32[4,128,1]{2,1,0:T(8,128)} %tile.13.ids_ref, bf16[1,2048]{1,0:T(2,128)(2,1)} %gain_ref.1, s32[192,1]{1,0:T(8,128)} %constant.6.clone.tgt_col_ref, s32[1,768]{1,0:T(1,128)} %constant.7.clone.tgt_row_ref, ...), custom_call_target="tpu_custom_call" | custom-call | tf_op jit(solution)/shard_map/layers/pallas_call | solution.py:389
  158.1 1.9 %copy.13 = bf16[1,4,32,2048]{3,2,1,0:T(8,128)(2,1)} copy(bf16[1,4,32,2048]{3,2,1,0:T(8,128)(2,1)} %layers.1) | data formatting | bytes 1048576

commit v2 on v1

--- a/solution.py
+++ b/solution.py
@@ -11,12 +11,15 @@
 MESH = pl.DeviceIdType.MESH
 EXPERTS = 4
 CHUNKS = 4
+GROUP = 4
+SHIFTS = [
+    *((2, 2), (1, 2), (2, 3), (1, 3)),
+    *((2, 1), (3, 2), (2, 0), (0, 2)),
+    *((1, 1), (3, 3), (1, 0), (0, 3)),
+    *((3, 1), (0, 1), (3, 0)),
+]
 F32 = jnp.float32
 BF16 = jnp.bfloat16
-
-
-def dist(shift, size):
-    return min(shift, size - shift)
 
 
 def wait_bytes(ref, sem):
@@ -49,6 +52,7 @@
     drecv,
     dother,
     rows,
+    squares,
     act,
     csend,
     crecv,
@@ -81,7 +85,7 @@
     half = width // 2
     chunk = half // CHUNKS
     hidden = wg.shape[1]
-    group = split * cap
+    group = GROUP * cap
     last = n_section - 1
     s = lax.axis_index("section")
     me = lax.axis_index("expert")
@@ -90,6 +94,7 @@
     ex, ey = me // split, me % split
     other = {"dp": zh * 2 + 1 - core}
     across = {"dp": (1 - zh) * 2 + core}
+    opposite = {"dp": (1 - zh) * 2 + 1 - core}
 
     mine = pl.ds(pl.multiple_of(core * half, half), half)
     theirs = pl.ds(pl.multiple_of((1 - core) * half, half), half)
@@ -106,13 +111,21 @@
     for load in loads:
         load.start()
 
-    shifts = sorted(
-        ((jx, jy) for jx in range(EXPERTS) for jy in range(split) if jx or jy),
-        key=lambda j: -dist(j[0], EXPERTS) - dist(j[1], split),
-    )
+    shifts = SHIFTS
+    turned = [(-jy % split, -jx % EXPERTS) for jx, jy in shifts]
+
+    def by_core(a, b):
+        return a + core * (b - a)
+
+    def sending(k):
+        (jx, jy), (kx, ky) = shifts[k], turned[k]
+        return by_core(k, shifts.index(turned[k])), by_core(jx, kx), by_core(jy, ky)
+
+    n_shift = len(shifts)
+    groups = (n_shift + 1) // GROUP
 
     def peer(jx, jy):
-        return {"expert": ((ex + jx) % EXPERTS) * split + (ey + jy) % split}
+        return {"expert": ((ex + jx + EXPERTS) % EXPERTS) * split + (ey + jy + split) % split}
 
     barrier = pltpu.get_barrier_semaphore()
 
@@ -130,6 +143,7 @@
         greet(peer(jx, jy))
     greet(other)
     greet(across)
+    greet(opposite)
 
     @pl.when(s < last)
     def _():
@@ -148,7 +162,9 @@
         n = CHUNKS * tok
         row = lax.broadcasted_iota(jnp.int32, (n, n), 0)
         col = lax.broadcasted_iota(jnp.int32, (n, n), 1)
-        ids_col = ids_ref[c]
+        token = lax.broadcasted_iota(jnp.int32, (n, tok), 0) % tok
+        listed = lax.broadcasted_iota(jnp.int32, (n, tok), 1)
+        ids_col = jnp.sum(jnp.where(token == listed, ids_ref[0, c], 0), axis=1, keepdims=True)
         ids_row = jnp.sum(jnp.where(row == col, ids_col, 0), axis=0, keepdims=True)
         same = (ids_col == ids_row) & (row // tok == col // tok)
         rank_row = jnp.sum((same & (row < col)).astype(jnp.int32), axis=0, keepdims=True)
@@ -162,7 +178,7 @@
 
     lax.fori_loop(0, spans, placement, 0)
 
-    expected = len(shifts) + 2 + 3 * (s < last).astype(jnp.int32) + 3 * (s > 0).astype(jnp.int32)
+    expected = len(shifts) + 3 + 3 * (s < last).astype(jnp.int32) + 3 * (s > 0).astype(jnp.int32)
     pl.semaphore_wait(barrier, expected)
 
     def remote(source, target, send_sem, recv_sem, device):
@@ -189,16 +205,18 @@
 
         sent = jnp.dot(place[c], hbuf[c], preferred_element_type=F32).astype(BF16)
         dsend[c] = sent.reshape(EXPERTS, CHUNKS * cap, chunk)
-        for jx, jy in shifts:
-            ix, iy = (-jx) % EXPERTS, (-jy) % split
+        for k in range(n_shift):
+            slot, jx, jy = sending(k)
             remote(
                 dsend.at[c, (ex + jx) % EXPERTS],
-                drecv.at[c, ix, iy],
+                drecv.at[c, slot],
                 dsend_sem.at[c],
-                drecv_sem.at[c, ix],
+                drecv_sem.at[c, k // GROUP],
                 peer(jx, jy),
             )
-        pltpu.make_async_copy(dsend.at[c, ex], drecv.at[c, 0, 0], drecv_sem.at[c, 0]).start()
+        pltpu.make_async_copy(
+            dsend.at[c, ex], drecv.at[c, n_shift], drecv_sem.at[c, groups - 1]
+        ).start()
 
         @pl.when(s > 0)
         def _():
@@ -215,7 +233,7 @@
 
     def unpack(source, i, side):
         z = jnp.dot(
-            perm_ref[...], source.reshape(split * CHUNKS * cap, chunk), preferred_element_type=F32
+            perm_ref[...], source.reshape(GROUP * CHUNKS * cap, chunk), preferred_element_type=F32
         )
         total = jnp.zeros((group, 1), F32)
         for q in range(CHUNKS):
@@ -226,18 +244,22 @@
             total = total + jnp.sum(part * part, axis=1, keepdims=True)
         return total
 
-    nearest = sorted(range(EXPERTS), key=lambda i: dist(i, EXPERTS))
+    def gather(c):
+        for i in range(groups):
+            here = pl.ds(i * GROUP, GROUP)
+            wait_bytes(drecv.at[c, here], drecv_sem.at[c, i])
+            remote(drecv.at[c, here], dother.at[c, here], fsend_sem.at[c], frecv_sem.at[c, i], other)
+            squares[i] = unpack(drecv[c, i * GROUP : (i + 1) * GROUP], i, 0)
+
+    def gather_other(c):
+        for i in range(groups):
+            here = pl.ds(i * GROUP, GROUP)
+            wait_bytes(dother.at[c, here], frecv_sem.at[c, i])
+            squares[i] = squares[i] + unpack(dother[c, i * GROUP : (i + 1) * GROUP], i, 1)
 
     def experts(c):
-        squares = [None] * EXPERTS
-        for i in nearest:
-            wait_bytes(drecv.at[c, i], drecv_sem.at[c, i])
-            remote(drecv.at[c, i], dother.at[c, i], fsend_sem.at[c], frecv_sem.at[c, i], other)
-            squares[i] = unpack(drecv[c, i], i, 0)
-        for i in nearest:
-            wait_bytes(dother.at[c, i], frecv_sem.at[c, i])
-            squares[i] = squares[i] + unpack(dother[c, i], i, 1)
-        scale = lax.rsqrt(jnp.concatenate(squares, axis=0) / width + 1e-5)
+        total = squares[...].reshape(groups * group, 1)
+        scale = lax.rsqrt(total / width + 1e-5)
         for j in range(hidden // 256):
             cols = slice(j * 256, (j + 1) * 256)
             gate = jnp.dot(rows[...], wg[:, cols], preferred_element_type=F32) * scale
@@ -247,32 +269,35 @@
             cols = slice(q * chunk, (q + 1) * chunk)
             csend[c, q] = jnp.dot(act[...], wd[1, :, cols], preferred_element_type=F32).astype(BF16)
             remote(csend.at[c, q], crecv.at[c, q], csend_sem.at[c], crecv_sem.at[c, q], other)
+
+    def down(c):
         for q in range(CHUNKS):
             cols = slice(q * chunk, (q + 1) * chunk)
             own[q] = jnp.dot(act[...], wd[0, :, cols], preferred_element_type=F32)
+
+    def give_back(c):
         for q in range(CHUNKS):
             wait_bytes(crecv.at[c, q], crecv_sem.at[c, q])
             both = (own[q] + crecv[c, q].astype(F32)).astype(BF16)
-            for i in range(EXPERTS):
+            for i in range(groups):
                 packed[i, q] = both[i * group : (i + 1) * group]
-        for i in reversed(nearest):
+        for i in range(groups):
             out = jnp.dot(
                 perm_t_ref[...],
                 packed[i].reshape(CHUNKS * group, chunk),
                 preferred_element_type=F32,
             ).astype(BF16)
-            rsend[c, i] = out.reshape(split, CHUNKS * cap, chunk)
-            for jx, jy in shifts:
-                if jx == i:
-                    iy = (-jy) % split
-                    remote(
-                        rsend.at[c, jx, jy],
-                        rrecv.at[c, ex, iy],
-                        rsend_sem.at[c],
-                        rrecv_sem.at[c],
-                        peer(jx, jy),
-                    )
-        pltpu.make_async_copy(rsend.at[c, 0, 0], rrecv.at[c, ex, 0], rrecv_sem.at[c]).start()
+            rsend[c, i * GROUP : (i + 1) * GROUP] = out.reshape(GROUP, CHUNKS * cap, chunk)
+            for k in range(i * GROUP, min(n_shift, (i + 1) * GROUP)):
+                slot, jx, jy = sending(k)
+                remote(
+                    rsend.at[c, slot],
+                    rrecv.at[c, ex, ey],
+                    rsend_sem.at[c],
+                    rrecv_sem.at[c],
+                    peer(-jx, -jy),
+                )
+        pltpu.make_async_copy(rsend.at[c, n_shift], rrecv.at[c, ex, ey], rrecv_sem.at[c]).start()
 
     def combine(c):
         wait_bytes(rrecv.at[c], rrecv_sem.at[c])
@@ -289,52 +314,57 @@
                     hrecv.at[c, zh],
                     hsend_sem.at[c],
                     hrecv_sem.at[c],
-                    {"section": s + 1, "dp": k * 2 + core},
+                    {"section": s + 1, "dp": (1 - zh if k == 0 else zh) * 2 + core},
                 )
 
         @pl.when(s == last)
         def _():
-            remote(hsend.at[c], zrecv.at[c], zsend_sem.at[c], zrecv_sem.at[c], across)
+            zrecv[c, d] = hsend[c]
+            for device in (across, opposite, other):
+                remote(
+                    hsend.at[c], zrecv.at[c, d], zsend_sem.at[c], zrecv_sem.at[c], device
+                )
 
     def finish(c):
-        wait_bytes(zrecv.at[c], zrecv_sem.at[c])
-        whole = (hsend[c].astype(F32) + zrecv[c].astype(F32)).astype(BF16)
-        for q in range(CHUNKS):
-            obuf[c, core, :, q * chunk : (q + 1) * chunk] = whole[q * tok : (q + 1) * tok]
-        remote(obuf.at[c, core], obuf.at[c, core], osend_sem.at[c], orecv_sem.at[c], other)
-
-    def tick(t, carry):
-        @pl.when(t < spans)
-        def _():
-            dispatch(t)
-
-        @pl.when(t == 1)
+        wait_bytes(zrecv.at[c, pl.ds(0, 3)], zrecv_sem.at[c])
+        for k in range(2):
+            whole = (zrecv[c, k].astype(F32) + zrecv[c, 2 + k].astype(F32)).astype(BF16)
+            for q in range(CHUNKS):
+                obuf[c, k, :, q * chunk : (q + 1) * chunk] = whole[q * tok : (q + 1) * tok]
+
+    def load_wait(c):
+        @pl.when(c == 0)
         def _():
             for load in loads:
                 load.wait()
 
-        @pl.when((t >= 1) & (t < spans + 1))
-        def _():
-            experts(t - 1)
-
-        @pl.when((t >= 2) & (t < spans + 2))
-        def _():
-            combine(t - 2)
-
-        @pl.when((t >= 3) & (s == last))
-        def _():
-            finish(t - 3)
-
+    def last_only(c):
+        @pl.when(s == last)
+        def _():
+            finish(c)
+
+    def step(t, lag, phase):
+        @pl.when((t >= lag) & (t < spans + lag))
+        def _():
+            phase(t - lag)
+
+    def tick(t, carry):
+        step(t, 1, gather)
+        step(t, 0, dispatch)
+        step(t, 1, gather_other)
+        step(t, 1, load_wait)
+        step(t, 1, experts)
+        step(t, 1, down)
+        step(t, 2, combine)
+        step(t, 1, give_back)
+        step(t, 3, last_only)
         return carry
 
     lax.fori_loop(0, spans + 3, tick, 0)
 
     def drain(c, carry):
-        everyone = pl.ds(0, split - 1)
-        wait_bytes(drecv.at[c, pl.ds(0, EXPERTS - 1)], dsend_sem.at[c])
-        wait_bytes(drecv.at[c, EXPERTS - 1, everyone], dsend_sem.at[c])
-        wait_bytes(drecv.at[c, pl.ds(0, EXPERTS - 1)], rsend_sem.at[c])
-        wait_bytes(drecv.at[c, EXPERTS - 1, everyone], rsend_sem.at[c])
+        wait_bytes(drecv.at[c, pl.ds(0, n_shift)], dsend_sem.at[c])
+        wait_bytes(drecv.at[c, pl.ds(0, n_shift)], rsend_sem.at[c])
         wait_bytes(drecv.at[c], fsend_sem.at[c])
         wait_bytes(csend.at[c], csend_sem.at[c])
 
@@ -345,9 +375,7 @@
 
         @pl.when(s == last)
         def _():
-            wait_bytes(hsend.at[c], zsend_sem.at[c])
-            wait_bytes(ostage.at[c], osend_sem.at[c])
-            wait_bytes(ostage.at[c], orecv_sem.at[c])
+            wait_bytes(zrecv.at[c, pl.ds(0, 3)], zsend_sem.at[c])
 
         @pl.when(s > 0)
         def _():
@@ -369,8 +397,8 @@
     cap = tok // EXPERTS * 3 // 2
     half = width // 2
     chunk = half // CHUNKS
-    group = split * cap
-    total = EXPERTS * group
+    group = GROUP * cap
+    total = n_expert * cap
     block = CHUNKS * cap
 
     stride = EXPERTS * cap
@@ -378,14 +406,13 @@
     key = (e * cap + r + stride * q).reshape(EXPERTS, block)
     tgt_col = key.reshape(-1, 1).astype(np.int32)
     tgt_row = np.repeat(key[:, None], split, axis=1).reshape(1, -1).astype(np.int32)
-    order = np.arange(split * block).reshape(split, CHUNKS, cap).transpose(1, 0, 2).reshape(-1)
-    perm = np.eye(split * block, dtype=np.float32)[order]
-    ids = jnp.tile(expert_ids[0], (1, CHUNKS, 1))
+    order = np.arange(GROUP * block).reshape(GROUP, CHUNKS, cap).transpose(1, 0, 2).reshape(-1)
+    perm = np.eye(GROUP * block, dtype=np.float32)[order]
 
     vmem = pl.BlockSpec(memory_space=pltpu.VMEM)
     hbm = pl.BlockSpec(memory_space=pl.ANY)
     dma = pltpu.SemaphoreType.DMA
-    blocks = (spans, EXPERTS, split, block, chunk)
+    blocks = (spans, n_expert, block, chunk)
     return pl.pallas_call(
         functools.partial(kernel, n_section, split, cap),
         out_shape=jax.ShapeDtypeStruct((1, spans, tok, width), BF16),
@@ -403,23 +430,24 @@
             pltpu.VMEM(blocks, BF16),
             pltpu.VMEM(blocks, BF16),
             pltpu.VMEM((total, width), BF16),
+            pltpu.VMEM((total // group, group, 1), F32),
             pltpu.VMEM((total, hidden), BF16),
             pltpu.VMEM((spans, CHUNKS, total, chunk), BF16),
             pltpu.VMEM((spans, CHUNKS, total, chunk), BF16),
             pltpu.VMEM((CHUNKS, total, chunk), F32),
-            pltpu.VMEM((EXPERTS, CHUNKS, group, chunk), BF16),
+            pltpu.VMEM((total // group, CHUNKS, group, chunk), BF16),
             pltpu.VMEM(blocks, BF16),
-            pltpu.VMEM(blocks, BF16),
+            pltpu.VMEM((spans, EXPERTS, split, block, chunk), BF16),
             pltpu.VMEM((spans, CHUNKS * tok, chunk), BF16),
             pltpu.VMEM((spans, 2, CHUNKS * tok, chunk), BF16),
-            pltpu.VMEM((spans, CHUNKS * tok, chunk), BF16),
+            pltpu.VMEM((spans, 4, CHUNKS * tok, chunk), BF16),
             pltpu.VMEM((spans, tok, half), BF16),
             pltpu.VMEM((spans, 2, tok, half), BF16),
             dma((6,)),
             dma((spans,)),
-            dma((spans, EXPERTS)),
-            dma((spans,)),
-            dma((spans, EXPERTS)),
+            dma((spans, total // group)),
+            dma((spans,)),
+            dma((spans, total // group)),
             dma((spans,)),
             dma((spans, CHUNKS)),
             dma((spans,)),
@@ -437,7 +465,7 @@
         name="layers",
     )(
         inputs,
-        ids,
+        jnp.swapaxes(expert_ids, 2, 3),
         norm_gain,
         jnp.asarray(tgt_col),
         jnp.asarray(tgt_row),

time: 160 us -> 151 us (0.944)
  Pallas kernels: 156 us -> 149 us
  local copies, waits for them, and re-layouts: 3.54 us -> 1.88 us
    pallas_call x1, Pallas kernels: 156 us -> 149 us  [shards(): pl.pallas_call(functools.partial(kernel, n_section, split, cap), out_shap...]
    another operation x2 -> x0, local copies, waits for them, and re-layouts: 1.66 us -> none  [shards(): ids = jnp.tile(expert_ids[0], (1, CHUNKS, 1))]
where the time goes in v2:
time: 151 us; the launch traced here: 150 us
  Pallas kernels  149 us (99%)
  local copies, waits for them, and re-layouts  1.88 us (1%)
    pallas_call x1, Pallas kernels, shards(): pl.pallas_call(functools.partial(kernel, n_section, split, cap), out_shap...  149 us

profile of v2, /device:TPU:97, one launch (start us, length us, event | category | flops | bytes accessed | tf_op | source)
XLA Modules:
  0.0 150.4 jit_solution(7829702951623582125)
XLA Ops:
  0.0 148.5 %layers.1 = bf16[1,4,32,2048]{3,2,1,0:T(8,128)(2,1)} custom-call(bf16[4,32,2048]{2,1,0:T(8,128)(2,1)} %x_ref.1, s32[1,4,1,32]{3,2,1,0:T(1,128)} %bitcast.3, bf16[1,2048]{1,0:T(2,128)(2,1)} %gain_ref.1, s32[192,1]{1,0:T(8,128)} %constant.6.clone.tgt_col_ref, s32[1,768]{1,0:T(1,128)} %constant.7.clone.tgt_row_ref, ...), custom_call_target="tpu_custom_call" | custom-call | tf_op jit(solution)/shard_map/layers/pallas_call | solution.py:416
  148.5 1.9 %copy.13 = bf16[1,4,32,2048]{3,2,1,0:T(8,128)(2,1)} copy(bf16[1,4,32,2048]{3,2,1,0:T(8,128)(2,1)} %layers.1) | data formatting | bytes 1048576

commit v3 on v2

--- a/solution.py
+++ b/solution.py
@@ -53,6 +53,7 @@
     dother,
     rows,
     squares,
+    sums,
     act,
     csend,
     crecv,
@@ -176,7 +177,7 @@
         place_t[c] = (tgt_row_ref[...] == key_col).astype(F32).astype(BF16)
         return carry
 
-    lax.fori_loop(0, spans, placement, 0)
+    placement(0, 0)
 
     expected = len(shifts) + 3 + 3 * (s < last).astype(jnp.int32) + 3 * (s > 0).astype(jnp.int32)
     pl.semaphore_wait(barrier, expected)
@@ -191,18 +192,7 @@
             device_id_type=MESH,
         ).start()
 
-    def dispatch(c):
-        @pl.when(s == 0)
-        def _():
-            for q in range(CHUNKS):
-                cols = pl.ds(pl.multiple_of(core * half + q * chunk, chunk), chunk)
-                hbuf[c, q * tok : (q + 1) * tok] = x_ref[c, :, cols]
-
-        @pl.when(s > 0)
-        def _():
-            wait_bytes(hrecv.at[c], hrecv_sem.at[c])
-            hbuf[c] = (hrecv[c, 0].astype(F32) + hrecv[c, 1].astype(F32)).astype(BF16)
-
+    def send_rows(c):
         sent = jnp.dot(place[c], hbuf[c], preferred_element_type=F32).astype(BF16)
         dsend[c] = sent.reshape(EXPERTS, CHUNKS * cap, chunk)
         for k in range(n_shift):
@@ -218,18 +208,26 @@
             dsend.at[c, ex], drecv.at[c, n_shift], drecv_sem.at[c, groups - 1]
         ).start()
 
-        @pl.when(s > 0)
-        def _():
-            for q in range(CHUNKS):
-                ostage[c, :, q * chunk : (q + 1) * chunk] = hbuf[c, q * tok : (q + 1) * tok]
-            for k in range(2):
-                remote(
-                    ostage.at[c],
-                    obuf.at[c, core],
-                    osend_sem.at[c],
-                    orecv_sem.at[c],
-                    {"section": s - 1, "dp": zh * 2 + k},
-                )
+    def dispatch_inputs(c):
+        for q in range(CHUNKS):
+            cols = pl.ds(pl.multiple_of(core * half + q * chunk, chunk), chunk)
+            hbuf[c, q * tok : (q + 1) * tok] = x_ref[c, :, cols]
+        send_rows(c)
+
+    def dispatch(c):
+        wait_bytes(hrecv.at[c], hrecv_sem.at[c])
+        hbuf[c] = (hrecv[c, 0].astype(F32) + hrecv[c, 1].astype(F32)).astype(BF16)
+        send_rows(c)
+        for q in range(CHUNKS):
+            ostage[c, :, q * chunk : (q + 1) * chunk] = hbuf[c, q * tok : (q + 1) * tok]
+        for k in range(2):
+            remote(
+                ostage.at[c],
+                obuf.at[c, core],
+                osend_sem.at[c],
+                orecv_sem.at[c],
+                {"section": s - 1, "dp": zh * 2 + k},
+            )
 
     def unpack(source, i, side):
         z = jnp.dot(
@@ -257,14 +255,29 @@
             wait_bytes(dother.at[c, here], frecv_sem.at[c, i])
             squares[i] = squares[i] + unpack(dother[c, i * GROUP : (i + 1) * GROUP], i, 1)
 
+    def experts_own(c):
+        for j in range(hidden // 256):
+            cols = slice(j * 256, (j + 1) * 256)
+            sums[0, :, cols] = jnp.dot(
+                rows[:, 0:half], wg[0:half, cols], preferred_element_type=F32
+            )
+            sums[1, :, cols] = jnp.dot(
+                rows[:, 0:half], wu[0:half, cols], preferred_element_type=F32
+            )
+
     def experts(c):
         total = squares[...].reshape(groups * group, 1)
         scale = lax.rsqrt(total / width + 1e-5)
         for j in range(hidden // 256):
             cols = slice(j * 256, (j + 1) * 256)
-            gate = jnp.dot(rows[...], wg[:, cols], preferred_element_type=F32) * scale
-            upper = jnp.dot(rows[...], wu[:, cols], preferred_element_type=F32) * scale
-            act[:, cols] = (gate / (1.0 + jnp.exp(-gate)) * upper).astype(BF16)
+            gate = sums[0, :, cols] + jnp.dot(
+                rows[:, half:width], wg[half:width, cols], preferred_element_type=F32
+            )
+            upper = sums[1, :, cols] + jnp.dot(
+                rows[:, half:width], wu[half:width, cols], preferred_element_type=F32
+            )
+            gate = gate * scale
+            act[:, cols] = (gate / (1.0 + jnp.exp(-gate)) * (upper * scale)).astype(BF16)
         for q in range(CHUNKS):
             cols = slice(q * chunk, (q + 1) * chunk)
             csend[c, q] = jnp.dot(act[...], wd[1, :, cols], preferred_element_type=F32).astype(BF16)
@@ -343,6 +356,22 @@
         def _():
             finish(c)
 
+    def later_section(phase):
+        def run(c):
+            @pl.when(s > 0)
+            def _():
+                phase(c)
+
+        return run
+
+    def first_section(phase):
+        def run(c):
+            @pl.when((s == 0) & (c >= 2))
+            def _():
+                phase(c)
+
+        return run
+
     def step(t, lag, phase):
         @pl.when((t >= lag) & (t < spans + lag))
         def _():
@@ -350,9 +379,11 @@
 
     def tick(t, carry):
         step(t, 1, gather)
-        step(t, 0, dispatch)
+        step(t, -1, first_section(dispatch_inputs))
+        step(t, 0, later_section(dispatch))
+        step(t, 1, load_wait)
+        step(t, 1, experts_own)
         step(t, 1, gather_other)
-        step(t, 1, load_wait)
         step(t, 1, experts)
         step(t, 1, down)
         step(t, 2, combine)
@@ -360,6 +391,15 @@
         step(t, 3, last_only)
         return carry
 
+    for c in range(2):
+
+        @pl.when(s == 0)
+        def _():
+            dispatch_inputs(c)
+
+        placement(c + 1, 0)
+
+    lax.fori_loop(3, spans, placement, 0)
     lax.fori_loop(0, spans + 3, tick, 0)
 
     def drain(c, carry):
@@ -431,6 +471,7 @@
             pltpu.VMEM(blocks, BF16),
             pltpu.VMEM((total, width), BF16),
             pltpu.VMEM((total // group, group, 1), F32),
+            pltpu.VMEM((2, total, hidden), F32),
             pltpu.VMEM((total, hidden), BF16),
             pltpu.VMEM((spans, CHUNKS, total, chunk), BF16),
             pltpu.VMEM((spans, CHUNKS, total, chunk), BF16),

time: 151 us -> 148 us (0.980)
  Pallas kernels: 149 us -> 146 us
    pallas_call x1, Pallas kernels: 149 us -> 146 us  [shards(): pl.pallas_call(functools.partial(kernel, n_section, split, cap), out_shap...]
where the time goes in v3:
time: 148 us
  Pallas kernels  146 us (99%)
  local copies, waits for them, and re-layouts  1.88 us (1%)
    pallas_call x1, Pallas kernels, shards(): pl.pallas_call(functools.partial(kernel, n_section, split, cap), out_shap...  146 us

profile of v3, /device:TPU:97, one launch (start us, length us, event | category | flops | bytes accessed | tf_op | source)
XLA Modules:
  0.0 147.7 jit_solution(7340497612906995306)
XLA Ops:
  0.0 145.8 %layers.1 = bf16[1,4,32,2048]{3,2,1,0:T(8,128)(2,1)} custom-call(bf16[4,32,2048]{2,1,0:T(8,128)(2,1)} %x_ref.1, s32[1,4,1,32]{3,2,1,0:T(1,128)} %bitcast.3, bf16[1,2048]{1,0:T(2,128)(2,1)} %gain_ref.1, s32[192,1]{1,0:T(8,128)} %constant.6.clone.tgt_col_ref, s32[1,768]{1,0:T(1,128)} %constant.7.clone.tgt_row_ref, ...), custom_call_target="tpu_custom_call" | custom-call | tf_op jit(solution)/shard_map/layers/pallas_call | solution.py:456
  145.8 1.9 %copy.13 = bf16[1,4,32,2048]{3,2,1,0:T(8,128)(2,1)} copy(bf16[1,4,32,2048]{3,2,1,0:T(8,128)(2,1)} %layers.1) | data formatting | bytes 1048576

commit v4 on v3

--- a/solution.py
+++ b/solution.py
@@ -256,8 +256,7 @@
             squares[i] = squares[i] + unpack(dother[c, i * GROUP : (i + 1) * GROUP], i, 1)
 
     def experts_own(c):
-        for j in range(hidden // 256):
-            cols = slice(j * 256, (j + 1) * 256)
+        for cols in (slice(0, hidden),):
             sums[0, :, cols] = jnp.dot(
                 rows[:, 0:half], wg[0:half, cols], preferred_element_type=F32
             )
@@ -268,8 +267,7 @@
     def experts(c):
         total = squares[...].reshape(groups * group, 1)
         scale = lax.rsqrt(total / width + 1e-5)
-        for j in range(hidden // 256):
-            cols = slice(j * 256, (j + 1) * 256)
+        for cols in (slice(0, hidden),):
             gate = sums[0, :, cols] + jnp.dot(
                 rows[:, half:width], wg[half:width, cols], preferred_element_type=F32
             )
@@ -277,7 +275,8 @@
                 rows[:, half:width], wu[half:width, cols], preferred_element_type=F32
             )
             gate = gate * scale
-            act[:, cols] = (gate / (1.0 + jnp.exp(-gate)) * (upper * scale)).astype(BF16)
+            gate = 0.5 * gate
+            act[:, cols] = (gate * (1.0 + jnp.tanh(gate)) * (upper * scale)).astype(BF16)
         for q in range(CHUNKS):
             cols = slice(q * chunk, (q + 1) * chunk)
             csend[c, q] = jnp.dot(act[...], wd[1, :, cols], preferred_element_type=F32).astype(BF16)

time: 148 us -> 148 us (level)
  no operation moved by 1% of the time
where the time goes in v4:
time: 148 us
  Pallas kernels  146 us (99%)
  local copies, waits for them, and re-layouts  1.88 us (1%)
    pallas_call x1, Pallas kernels, shards(): pl.pallas_call(functools.partial(kernel, n_section, split, cap), out_shap...  146 us

profile of v4, /device:TPU:97, one launch (start us, length us, event | category | flops | bytes accessed | tf_op | source)
XLA Modules:
  0.0 148.2 jit_solution(1715100801426624031)
XLA Ops:
  0.0 146.3 %layers.1 = bf16[1,4,32,2048]{3,2,1,0:T(8,128)(2,1)} custom-call(bf16[4,32,2048]{2,1,0:T(8,128)(2,1)} %x_ref.1, s32[1,4,1,32]{3,2,1,0:T(1,128)} %bitcast.3, bf16[1,2048]{1,0:T(2,128)(2,1)} %gain_ref.1, s32[192,1]{1,0:T(8,128)} %constant.6.clone.tgt_col_ref, s32[1,768]{1,0:T(1,128)} %constant.7.clone.tgt_row_ref, ...), custom_call_target="tpu_custom_call" | custom-call | tf_op jit(solution)/shard_map/layers/pallas_call | solution.py:455
  146.3 1.9 %copy.13 = bf16[1,4,32,2048]{3,2,1,0:T(8,128)(2,1)} copy(bf16[1,4,32,2048]{3,2,1,0:T(8,128)(2,1)} %layers.1) | data formatting | bytes 1048576

commit v5 on v3

--- a/solution.py
+++ b/solution.py
@@ -244,13 +244,20 @@
 
     def gather(c):
         for i in range(groups):
+            if i == groups - 1:
+                take_other(c, 0, early)
             here = pl.ds(i * GROUP, GROUP)
             wait_bytes(drecv.at[c, here], drecv_sem.at[c, i])
             remote(drecv.at[c, here], dother.at[c, here], fsend_sem.at[c], frecv_sem.at[c, i], other)
             squares[i] = unpack(drecv[c, i * GROUP : (i + 1) * GROUP], i, 0)
 
     def gather_other(c):
-        for i in range(groups):
+        take_other(c, early, groups)
+
+    early = groups - 2
+
+    def take_other(c, begin, end):
+        for i in range(begin, end):
             here = pl.ds(i * GROUP, GROUP)
             wait_bytes(dother.at[c, here], frecv_sem.at[c, i])
             squares[i] = squares[i] + unpack(dother[c, i * GROUP : (i + 1) * GROUP], i, 1)

time: 148 us -> 146 us (0.986)
  Pallas kernels: 146 us -> 144 us
    pallas_call x1, Pallas kernels: 146 us -> 144 us  [shards(): pl.pallas_call(functools.partial(kernel, n_section, split, cap), out_shap...]
where the time goes in v5:
time: 146 us
  Pallas kernels  144 us (99%)
  local copies, waits for them, and re-layouts  1.88 us (1%)
    pallas_call x1, Pallas kernels, shards(): pl.pallas_call(functools.partial(kernel, n_section, split, cap), out_shap...  144 us

profile of v5, /device:TPU:97, one launch (start us, length us, event | category | flops | bytes accessed | tf_op | source)
XLA Modules:
  0.0 145.9 jit_solution(407003565735518893)
XLA Ops:
  0.0 144.0 %layers.1 = bf16[1,4,32,2048]{3,2,1,0:T(8,128)(2,1)} custom-call(bf16[4,32,2048]{2,1,0:T(8,128)(2,1)} %x_ref.1, s32[1,4,1,32]{3,2,1,0:T(1,128)} %bitcast.3, bf16[1,2048]{1,0:T(2,128)(2,1)} %gain_ref.1, s32[192,1]{1,0:T(8,128)} %constant.6.clone.tgt_col_ref, s32[1,768]{1,0:T(1,128)} %constant.7.clone.tgt_row_ref, ...), custom_call_target="tpu_custom_call" | custom-call | tf_op jit(solution)/shard_map/layers/pallas_call | solution.py:463
  144.0 1.9 %copy.13 = bf16[1,4,32,2048]{3,2,1,0:T(8,128)(2,1)} copy(bf16[1,4,32,2048]{3,2,1,0:T(8,128)(2,1)} %layers.1) | data formatting | bytes 1048576
